TPU v7x, 128 devices: a whole 4x4x4 slice. The times are simulated.
128 devices in a mesh: wide: 32 (over y, z, core), narrow: 4 (over x).
Axes of the slice: x: 4, y: 4, z: 4, core: 2. Of those that a mesh axis runs over, the one named last changes fastest.
Arguments:
- superheat_excess: float32 [128, 512, 512], P('wide', 'narrow'), may hold values from -6 to 6
- liquid_indicator: int32 [128, 512, 512], P('wide', 'narrow'), may hold values from 0 to 1, as said below
- group_patch_listing_table: int32 [32, 4, 16], P('wide', 'narrow'), may hold values from -1 to 31, as said below
- source_smearing_factors_north: float32 [16, 16], replicated, may hold values from 0 to 2, as said below
- source_smearing_factors_east: float32 [128, 128], replicated, may hold values from 0 to 2, as said below
Outputs:
- temperature_next: float32 [128, 512, 512], P('wide', 'narrow')
- pressure: float32 [128, 512, 512], P('wide', 'narrow')
- residual: float32 [128, 512, 512], P('wide', 'narrow')
Inputs may be any that keep to these rules, and one draw needn't show every extreme that they name: In each row group_patch_listing_table[w, n] the listed tile numbers come first and are distinct, the remaining entries are -1. A row lists 1 to 16 tiles; for every w the rows n < 4 list exactly 32 tiles together, and one of them lists 16. `liquid_indicator`: phase is 1 in every cell outside the listed tiles. `source_smearing_factors_north`: the identity plus entries drawn in 0 to 1.2 / 16. `source_smearing_factors_east`: the identity plus entries drawn in 0 to 1.2 / 128.
All inputs are finite; a program needn't handle non-finite values.
Results may differ from a plain program's by a relative error of at most 0.0003.
Values sent between devices are 32-bit elements; how exact they have to be, the bound alone decides.
A program may use at most 64 MiB of HBM per device.

v0:
```python
import math
import jax
import jax.numpy as jnp
from jax import lax
from jax.sharding import Mesh
from jax.sharding import PartitionSpec as P

ITERS = 3
WIDE_NARROW = ("wide_0", "wide_1", "wide_2", "narrow")
WIDE = ("wide_0", "wide_1", "wide_2")
conduct_liquid = 1.0
conduct_vapor = 0.4
diffusion = 0.06
mobility_liquid = 1.0
mobility_vapor = 4.0
expansion = 0.3
compress = 0.01
highest = lax.Precision.HIGHEST


def padded_2(array, sides, width):
    edges = {}
    for axis, dim in sides:
        devices, length = (lax.axis_size(axis), array.shape[dim])
        up = [(i, (i + 1) % devices) for i in range(devices - 1)]
        last = lax.slice_in_dim(array, length - width, length, axis=dim)
        initial = lax.slice_in_dim(array, 0, width, axis=dim)
        edges[dim] = (
            lax.ppermute(last, axis, up),
            lax.ppermute(initial, axis, [(b, a) for a, b in up]),
        )
    done = []
    for _, dim in sides:
        low, high = edges[dim]
        around = [(width, width) if d in done else (0, 0) for d in range(array.ndim)]
        array = jnp.concatenate([jnp.pad(low, around), array, jnp.pad(high, around)], axis=dim)
        done.append(dim)
    return array


def over_axes(array, axes):
    for axis in axes:
        array = lax.psum(array, axis)
    return array


def centre(padded):
    return padded[1:-1, 1:-1, 1:-1]


def neighbours(padded):
    return [
        padded[2:, 1:-1, 1:-1],
        padded[:-2, 1:-1, 1:-1],
        padded[1:-1, 2:, 1:-1],
        padded[1:-1, :-2, 1:-1],
        padded[1:-1, 1:-1, 2:],
        padded[1:-1, 1:-1, :-2],
    ]


def heat_advance(temp_pad, liquid_indicator_haloed, inner_region_haloed):
    current = centre(temp_pad)
    phases = centre(liquid_indicator_haloed)
    conduct = jnp.where(phases > 0.5, conduct_liquid, conduct_vapor)
    flux = jnp.zeros_like(current)
    faces = jnp.zeros_like(current)
    for near_temp, near_phase, near_inside in zip(
        neighbours(temp_pad), neighbours(liquid_indicator_haloed), neighbours(inner_region_haloed)
    ):
        differ = jnp.abs(near_phase - phases) > 0.5
        flux = flux + near_inside * jnp.where(differ, -2.0 * current, near_temp - current)
        faces = faces + near_inside * jnp.where(differ, 1.0, 0.0)
    heated_values = current + diffusion * conduct * flux
    vaporised_amount = 2.0 * conduct * faces * heated_values
    return (heated_values, vaporised_amount)


def face_weights(liquid_indicator_haloed, inner_region_haloed):
    mobility = jnp.where(liquid_indicator_haloed > 0.5, mobility_liquid, mobility_vapor)
    own = centre(mobility)
    return [
        near_inside * 0.5 * (own + near_mob)
        for near_inside, near_mob in zip(neighbours(inner_region_haloed), neighbours(mobility))
    ]


def apply_operator(field_pad, weights):
    field = centre(field_pad)
    total = compress * field
    for weight, near in zip(weights, neighbours(field_pad)):
        total = total + weight * (field - near)
    return total


def smear_tiles(tiles, source_smearing_factors_north, source_smearing_factors_east):
    across = jnp.einsum("...bc,dc->...bd", tiles, source_smearing_factors_east, precision=highest)
    return expansion * jnp.einsum(
        "ab,...bd->...ad", source_smearing_factors_north, across, precision=highest
    )


def cosine_rows(extent, klength, clength):
    waves = jnp.arange(klength, dtype=jnp.int32)
    centres = 2 * jnp.arange(clength, dtype=jnp.int32) + 1
    turns = waves[:, None] * centres[None, :] % (4 * extent)
    angles = 2.0 * math.pi / (4 * extent) * turns.astype(jnp.float32)
    scales = jnp.where(waves == 0, math.sqrt(1.0 / extent), math.sqrt(2.0 / extent)).astype(
        jnp.float32
    )
    return scales[:, None] * jnp.cos(angles)


def eigen(extent, first, length):
    waves = (first + jnp.arange(length, dtype=jnp.int32)).astype(jnp.float32)
    return 4.0 * jnp.sin(waves * (math.pi / (2 * extent))) ** 2


def inside_range(first, length, limit):
    places = first + jnp.arange(length, dtype=jnp.int32)
    return jnp.logical_and(places >= 0, places < limit).astype(jnp.float32)


def padded_field(field):
    rimmed = padded_2(field, ((WIDE, 0), ("narrow", 1)), 1)
    return jnp.pad(rimmed, ((0, 0), (0, 0), (1, 1)))


def inner(first_field, second_field):
    return over_axes(jnp.sum(first_field * second_field), WIDE_NARROW)


def on_device(
    superheat_excess,
    liquid_indicator,
    group_patch_listing_table,
    source_smearing_factors_north,
    source_smearing_factors_east,
):
    sheet_thickness, north_line_total, patch_span_east = superheat_excess.shape
    wide_count = lax.axis_size(WIDE)
    lanes = lax.axis_size("narrow")
    wide_index = lax.axis_index(WIDE)
    lane_index = lax.axis_index("narrow")
    total_y = north_line_total * lanes
    total_z = sheet_thickness * wide_count
    gathered_patches = jnp.stack([superheat_excess, liquid_indicator.astype(jnp.float32)])
    rimmed = padded_2(gathered_patches, ((WIDE, 1), ("narrow", 2)), 1)
    rimmed = jnp.pad(rimmed, ((0, 0), (0, 0), (0, 0), (1, 1)))
    z_inside = inside_range(wide_index * sheet_thickness - 1, sheet_thickness + 2, total_z)
    y_inside = inside_range(lane_index * north_line_total - 1, north_line_total + 2, total_y)
    x_inside = inside_range(-1, patch_span_east + 2, patch_span_east)
    inner_region_haloed = (
        z_inside[:, None, None] * y_inside[None, :, None] * x_inside[None, None, :]
    )
    heated_values, vaporised_amount = heat_advance(rimmed[0], rimmed[1], inner_region_haloed)
    flat_ids = group_patch_listing_table.reshape(-1)
    most = flat_ids.shape[0]
    size_y = source_smearing_factors_north.shape[0]
    size_x = source_smearing_factors_east.shape[0]
    tiles_y = north_line_total // size_y
    tiles_x = patch_span_east // size_x
    count_tiles = tiles_y * tiles_x
    blocks = vaporised_amount.reshape(sheet_thickness, tiles_y, size_y, tiles_x, size_x).transpose(
        1, 3, 0, 2, 4
    )
    blocks = blocks.reshape(count_tiles, sheet_thickness * size_y * size_x)
    listed = flat_ids >= 0
    numbers = jnp.arange(count_tiles, dtype=jnp.int32)
    choose = jnp.logical_and(flat_ids[:, None] == numbers[None, :], listed[:, None]).astype(
        jnp.float32
    )
    picked = jnp.dot(choose, blocks, precision=highest)
    smeared = smear_tiles(
        picked.reshape(most, sheet_thickness, size_y, size_x),
        source_smearing_factors_north,
        source_smearing_factors_east,
    ).reshape(most, -1)
    sourced = jnp.dot(choose.T, smeared, precision=highest)
    source = sourced.reshape(tiles_y, tiles_x, sheet_thickness, size_y, size_x).transpose(
        2, 0, 3, 1, 4
    )
    source = source.reshape(sheet_thickness, north_line_total, patch_span_east)
    table_x = cosine_rows(patch_span_east, patch_span_east, patch_span_east)
    table_z = cosine_rows(total_z, total_z, total_z)
    eigen_z = eigen(total_z, 0, total_z)
    table_y = cosine_rows(total_y, total_y, total_y).reshape(total_y, lanes, north_line_total)
    table_zw = table_z.reshape(total_z, wide_count, sheet_thickness)
    part_k = patch_span_east // (wide_count * lanes)
    eigen_y = eigen(total_y, 0, total_y)
    eigen_x = eigen(patch_span_east, (wide_index * lanes + lane_index) * part_k, part_k)

    def precondition(remainder):
        spectrum = jnp.einsum("zyx,kx->zyk", remainder, table_x, precision=highest)
        planes = lax.all_to_all(
            spectrum[None], WIDE_NARROW, split_axis=3, concat_axis=0, tiled=True
        )
        planes = planes.reshape(wide_count, lanes, sheet_thickness, north_line_total, part_k)
        planes = jnp.einsum("wnzyk,mwz->mnyk", planes, table_zw, precision=highest)
        planes = jnp.einsum("mnyk,lny->mlk", planes, table_y, precision=highest)
        denom = eigen_z[:, None, None] + eigen_y[None, :, None] + eigen_x[None, None, :] + compress
        planes = jnp.einsum("mlk,lny->mnyk", planes / denom, table_y, precision=highest)
        planes = jnp.einsum("mnyk,mwz->wnzyk", planes, table_zw, precision=highest)
        planes = planes.reshape(wide_count * lanes, sheet_thickness, north_line_total, part_k)
        slabs = lax.all_to_all(planes, WIDE_NARROW, split_axis=0, concat_axis=3, tiled=True)
        return jnp.einsum("zyk,kx->zyx", slabs[0], table_x, precision=highest)

    weights = face_weights(rimmed[1], inner_region_haloed)
    pressure = jnp.zeros_like(source)
    residual = source
    search = precondition(residual)
    aligned = inner(residual, search)
    direction = search
    for iteration in range(ITERS):
        image = apply_operator(padded_field(direction), weights)
        alpha = aligned / over_axes(jnp.sum(direction * image), WIDE_NARROW)
        pressure = pressure + alpha * direction
        residual = residual - alpha * image
        if iteration + 1 < ITERS:
            search = precondition(residual)
            renewed = inner(residual, search)
            direction = search + renewed / aligned * direction
            aligned = renewed
    return (heated_values, pressure, residual)


def solution(mesh):
    torus = Mesh(
        mesh.devices.reshape(4, 4, 2, mesh.shape["narrow"]),
        ("wide_0", "wide_1", "wide_2", "narrow"),
    )
    placed = (P(WIDE, "narrow", None), P(WIDE, "narrow", None), P(WIDE, "narrow", None), P(), P())
    return jax.shard_map(
        on_device,
        mesh=torus,
        in_specs=placed,
        out_specs=(P(WIDE, "narrow", None), P(WIDE, "narrow", None), P(WIDE, "narrow", None)),
        check_vma=False,
    )
```

profile of v0, /device:TPU:34, one launch (start us, length us, event | category | flops | bytes accessed | tf_op | source)
XLA Modules:
  0.0 524.9 jit_solution(13043440437132954281)
XLA Ops:
  2.3 3.4 collective-permute-start
  11.1 3.6 collective-permute-start.2
  15.1 4.8 collective-permute-done.1
  27.2 4.9 fusion.6
  44.3 7.0 %convolution_bitcast_fusion.15 = f32[1,4,128,512]{3,2,1,0:T(8,128)} fusion(f32[4,128,512]{2,1,0:T(8,128)S(1)} %reshape.309, s32[512]{0:T(512)S(1)} %multiply_add_fusion.3, f32[512]{0:T(512)S(1)} %fusion.261), kind=kOutput, calls=%fused_computation.47 | convolution fusion | flops 1614544896 | bytes 2101248 | tf_op jit(solution)/shard_map/zyx,kx->zyk/dot_general | solution.py:194
  53.9 12.1 %all-to-all-start = ((f32[1,4,128,512]{2,1,0,3:T(4,128)}), f32[1,4,128,512]{2,1,0,3:T(4,128)S(1)}, u32[]{:S(2)}, u32[]{:S(2)}) async-start(f32[1,4,128,512]{2,1,0,3:T(4,128)} %copy.65), calls=%async_computation | async-start | bytes 2097152 | tf_op jit(solution)/shard_map/all_to_all | solution.py:195
  66.3 17.5 %all-to-all-done = f32[1,4,128,512]{2,1,0,3:T(4,128)S(1)} async-done(((f32[1,4,128,512]{2,1,0,3:T(4,128)}), f32[1,4,128,512]{2,1,0,3:T(4,128)S(1)}, u32[]{:S(2)}, u32[]{:S(2)}) %all-to-all-start) | async-done | bytes 1048608 | tf_op jit(solution)/shard_map/all_to_all | solution.py:195
  85.4 7.2 %convolution_bitcast_fusion.13 = f32[128,512,4]{0,1,2:T(8,128)S(1)} fusion(f32[128,4,128,4]{2,0,1,3:T(8,128)S(1)} %convolution_bitcast_fusion.14, s32[4,128]{1,0:T(4,128)S(1)} %multiply_add_fusion.4, f32[512]{0:T(512)S(1)} %fusion.261), kind=kOutput, calls=%fused_computation.45 | convolution fusion | flops 1614544896 | bytes 2101248 | tf_op jit(solution)/shard_map/mnyk,lny->mlk/dot_general | solution.py:200
  92.7 6.3 %convolution_bitcast_fusion.12 = f32[128,4,128,4,1]{0,2,3,1,4:T(8,128)S(1)} fusion(f32[128,512,4]{0,1,2:T(8,128)S(1)} %convolution_bitcast_fusion.13, f32[4]{0:T(128)S(1)} %multiply_multiply_fusion.1, f32[128,512]{0,1:T(8,128)S(1)} %broadcast_add_fusion, s32[4,128]{1,0:T(4,128)S(1)} %multiply_add_fusion.4, f32[512]{0:T(512)S(1)} %fusion.261), kind=kOutput, calls=%fused_computation.44 | convolution fusion | flops 1615331328 | bytes 2363408 | tf_op jit(solution)/shard_map/mlk,lny->mnyk/dot_general | solution.py:202
  101.7 23.1 %all_to_all.90 = f32[128,4,128,4]{2,3,1,0:T(4,128)S(1)} all-to-all(f32[128,4,128,4]{2,3,1,0:T(4,128)S(1)} %copy.74), channel_id=1, replica_groups=mesh['wide_0'=4,'wide_1'=4,'wide_2'=2,'narrow'=4] {'wide_0','wide_1','wi..., dimensions={0} | all-to-all | bytes 2097152 | tf_op jit(solution)/shard_map/all_to_all | solution.py:205
  125.0 5.8 %fusion.126 = f32[4,128,512]{2,1,0:T(8,128)S(1)} fusion(f32[4,128,512]{1,2,0:T(8,128)S(1)} %bitcast.221, s32[512]{0:T(512)S(1)} %multiply_add_fusion.3, f32[512]{0:T(512)S(1)} %fusion.261), kind=kOutput, calls=%fused_computation.235 | convolution fusion | flops 1614544896 | bytes 2101248 | tf_op jit(solution)/shard_map/zyk,kx->zyx/dot_general | solution.py:206
  132.8 3.6 collective-permute-start.4
  138.6 3.7 collective-permute-start.6
  144.9 7.6 %multiply_reduce_fusion.4 = (f32[]{:T(128)}, f32[]{:T(128)}, f32[4,128,512]{2,1,0:T(8,128)}, f32[4,128,512]{2,1,0:T(8,128)}, f32[4,128,512]{2,1,0:T(8,128)}, /*i...) fusion(f32[4,128,512]{2,1,0:T(8,128)S(1)} %fusion.126, ...), kind=kLoop, calls=%fused_computation.222 | loop fusion | flops 12845054 | bytes 25714696 | tf_op jit(solution)/shard_map/reduce_sum | solution.py:216
  152.5 9.3 %all-reduce.14 = (f32[]{:T(128)}, f32[]{:T(128)}) all-reduce(f32[]{:T(128)} %get-tuple-element.4, f32[]{:T(128)} %get-tuple-element.3), channel_id=1, replica_groups=mesh['wide_0'=4,'wide_1'=4,'wide_2'=2,'narrow'=4] {'wide_0'}, use_global_device_ids=true, to_apply=%region_1.2 | all-reduce | flops 2 | bytes 16 | tf_op jit(solution)/shard_map/psum | solution.py:43
  161.8 12.1 %all-reduce.13 = (f32[]{:T(128)}, f32[]{:T(128)}) all-reduce(f32[]{:T(128)} %get-tuple-element.9, f32[]{:T(128)} %get-tuple-element.10), channel_id=1, replica_groups=mesh['wide_0'=4,'wide_1'=4,'wide_2'=2,'narrow'=4] {'wide_1'}, use_global_device_ids=true, to_apply=%region_2.3 | all-reduce | flops 2 | bytes 16 | tf_op jit(solution)/shard_map/psum | solution.py:43
  173.9 3.1 all-reduce.15
  177.0 10.0 %all-reduce.12 = (f32[]{:T(128)}, f32[]{:T(128)}) all-reduce(f32[]{:T(128)} %get-tuple-element.11, f32[]{:T(128)} %get-tuple-element.12), channel_id=1, replica_groups=mesh['wide_0'=4,'wide_1'=4,'wide_2'=2,'narrow'=4] {'narrow'}, use_global_device_ids=true, to_apply=%region_4.5 | all-reduce | flops 2 | bytes 16 | tf_op jit(solution)/shard_map/psum | solution.py:43
  190.0 6.8 %convolution_bitcast_fusion.10 = f32[1,4,128,512]{3,2,1,0:T(8,128)} fusion(f32[4,128,512]{2,1,0:T(8,128)S(1)} %multiply_subtract_fusion.2, s32[512]{0:T(512)S(1)} %multiply_add_fusion.3, f32[512]{0:T(512)S(1)} %fusion.261), kind=kOutput, calls=%fused_computation.42 | convolution fusion | flops 1614544896 | bytes 2101248 | tf_op jit(solution)/shard_map/zyx,kx->zyk/dot_general | solution.py:194
  198.4 21.8 %all_to_all.91 = f32[1,4,128,512]{2,1,0,3:T(4,128)S(1)} all-to-all(f32[1,4,128,512]{2,1,0,3:T(4,128)S(1)} %copy.77), channel_id=1, replica_groups=mesh['wide_0'=4,'wide_1'=4,'wide_2'=2,'narrow'=4] {'wide_0','wide_1','wi..., dimensions={3} | all-to-all | bytes 2097152 | tf_op jit(solution)/shard_map/all_to_all | solution.py:195
  221.9 7.2 %convolution_bitcast_fusion.8 = f32[128,512,4]{0,1,2:T(8,128)S(1)} fusion(f32[128,4,128,4]{2,0,1,3:T(8,128)S(1)} %convolution_bitcast_fusion.9, s32[4,128]{1,0:T(4,128)S(1)} %multiply_add_fusion.4, f32[512]{0:T(512)S(1)} %fusion.261), kind=kOutput, calls=%fused_computation.40 | convolution fusion | flops 1614544896 | bytes 2101248 | tf_op jit(solution)/shard_map/mnyk,lny->mlk/dot_general | solution.py:200
  229.2 6.0 %convolution_bitcast_fusion.7 = f32[128,4,128,4,1]{0,2,3,1,4:T(8,128)S(1)} fusion(f32[128,512,4]{0,1,2:T(8,128)S(1)} %convolution_bitcast_fusion.8, f32[4]{0:T(128)S(1)} %multiply_multiply_fusion.1, f32[128,512]{0,1:T(8,128)S(1)} %broadcast_add_fusion, s32[4,128]{1,0:T(4,128)S(1)} %multiply_add_fusion.4, f32[512]{0:T(512)S(1)} %fusion.261), kind=kOutput, calls=%fused_computation.39 | convolution fusion | flops 1615331328 | bytes 2363408 | tf_op jit(solution)/shard_map/mlk,lny->mnyk/dot_general | solution.py:202
  237.9 22.9 %all_to_all.92 = f32[128,4,128,4]{2,3,1,0:T(4,128)S(1)} all-to-all(f32[128,4,128,4]{2,3,1,0:T(4,128)S(1)} %copy.86), channel_id=1, replica_groups=mesh['wide_0'=4,'wide_1'=4,'wide_2'=2,'narrow'=4] {'wide_0','wide_1','wi..., dimensions={0} | all-to-all | bytes 2097152 | tf_op jit(solution)/shard_map/all_to_all | solution.py:205
  261.1 6.6 %multiply_reduce_fusion.3 = (f32[]{:T(128)}, f32[4,128,512]{2,1,0:T(8,128)S(1)}) fusion(f32[4,128,512]{2,1,0:T(8,128)S(1)} %multiply_subtract_fusion.2, f32[4,128,512]{1,2,0:T(8,128)S(1)} %bitcast.220, s32[512]{0:T(512)S(1)} %multiply_add_fusion.3, f32[512]{0:T(512)S(1)} %fusion.261), kind=kOutput, calls=%fused_computation.219 | convolution fusion | flops 1615069184 | bytes 3149828 | tf_op jit(solution)/shard_map/zyk,kx->zyx/dot_general | solution.py:206
  267.6 9.4 %psum.176 = f32[]{:T(128)} all-reduce(f32[]{:T(128)} %get-tuple-element.51), channel_id=1, replica_groups=mesh['wide_0'=4,'wide_1'=4,'wide_2'=2,'narrow'=4] {'wide_0'}, use_global_device_ids=true, to_apply=%region_11.12 | all-reduce | flops 1 | bytes 8 | tf_op jit(solution)/shard_map/psum | solution.py:43
  277.1 9.5 %psum.177 = f32[]{:T(128)} all-reduce(f32[]{:T(128)} %psum.176), channel_id=1, replica_groups=mesh['wide_0'=4,'wide_1'=4,'wide_2'=2,'narrow'=4] {'wide_1'}, use_global_device_ids=true, to_apply=%region_12.13 | all-reduce | flops 1 | bytes 8 | tf_op jit(solution)/shard_map/psum | solution.py:43
  289.7 9.8 %psum.179 = f32[]{:T(128)} all-reduce(f32[]{:T(128)} %psum.178), channel_id=1, replica_groups=mesh['wide_0'=4,'wide_1'=4,'wide_2'=2,'narrow'=4] {'narrow'}, use_global_device_ids=true, to_apply=%region_14.15 | all-reduce | flops 1 | bytes 8 | tf_op jit(solution)/shard_map/psum | solution.py:43
  303.2 3.6 collective-permute-start.8
  309.2 3.5 collective-permute-start.10
  317.8 9.3 %psum.180 = f32[]{:T(128)} all-reduce(f32[]{:T(128)} %get-tuple-element.15), channel_id=1, replica_groups=mesh['wide_0'=4,'wide_1'=4,'wide_2'=2,'narrow'=4] {'wide_0'}, use_global_device_ids=true, to_apply=%region_16.17 | all-reduce | flops 1 | bytes 8 | tf_op jit(solution)/shard_map/psum | solution.py:43
  327.1 10.9 %psum.181 = f32[]{:T(128)} all-reduce(f32[]{:T(128)} %psum.180), channel_id=1, replica_groups=mesh['wide_0'=4,'wide_1'=4,'wide_2'=2,'narrow'=4] {'wide_1'}, use_global_device_ids=true, to_apply=%region_17.18 | all-reduce | flops 1 | bytes 8 | tf_op jit(solution)/shard_map/psum | solution.py:43
  341.0 10.3 %psum.183 = f32[]{:T(128)} all-reduce(f32[]{:T(128)} %psum.182), channel_id=1, replica_groups=mesh['wide_0'=4,'wide_1'=4,'wide_2'=2,'narrow'=4] {'narrow'}, use_global_device_ids=true, to_apply=%region_19.20 | all-reduce | flops 1 | bytes 8 | tf_op jit(solution)/shard_map/psum | solution.py:43
  355.1 6.8 %convolution_bitcast_fusion.5 = f32[1,4,128,512]{3,2,1,0:T(8,128)} fusion(f32[4,128,512]{2,1,0:T(8,128)S(1)} %multiply_subtract_fusion.1, s32[512]{0:T(512)S(1)} %multiply_add_fusion.3, f32[512]{0:T(512)S(1)} %fusion.261), kind=kOutput, calls=%fused_computation.37 | convolution fusion | flops 1614544896 | bytes 2101248 | tf_op jit(solution)/shard_map/zyx,kx->zyk/dot_general | solution.py:194
  363.4 21.8 %all_to_all.93 = f32[1,4,128,512]{2,1,0,3:T(4,128)S(1)} all-to-all(f32[1,4,128,512]{2,1,0,3:T(4,128)S(1)} %copy.89), channel_id=1, replica_groups=mesh['wide_0'=4,'wide_1'=4,'wide_2'=2,'narrow'=4] {'wide_0','wide_1','wi..., dimensions={3} | all-to-all | bytes 2097152 | tf_op jit(solution)/shard_map/all_to_all | solution.py:195
  386.9 7.2 %convolution_bitcast_fusion.3 = f32[128,512,4]{0,1,2:T(8,128)S(1)} fusion(f32[128,4,128,4]{2,0,1,3:T(8,128)S(1)} %convolution_bitcast_fusion.4, s32[4,128]{1,0:T(4,128)S(1)} %multiply_add_fusion.4, f32[512]{0:T(512)S(1)} %fusion.261), kind=kOutput, calls=%fused_computation.35 | convolution fusion | flops 1614544896 | bytes 2101248 | tf_op jit(solution)/shard_map/mnyk,lny->mlk/dot_general | solution.py:200
  394.2 6.0 %convolution_bitcast_fusion.2 = f32[128,4,128,4,1]{0,2,3,1,4:T(8,128)S(1)} fusion(f32[128,512,4]{0,1,2:T(8,128)S(1)} %convolution_bitcast_fusion.3, f32[4]{0:T(128)S(1)} %multiply_multiply_fusion.1, f32[128,512]{0,1:T(8,128)S(1)} %broadcast_add_fusion, s32[4,128]{1,0:T(4,128)S(1)} %multiply_add_fusion.4, f32[512]{0:T(512)S(1)} %fusion.261), kind=kOutput, calls=%fused_computation.34 | convolution fusion | flops 1615331328 | bytes 2363408 | tf_op jit(solution)/shard_map/mlk,lny->mnyk/dot_general | solution.py:202
  403.0 23.1 %all_to_all.94 = f32[128,4,128,4]{2,3,1,0:T(4,128)S(1)} all-to-all(f32[128,4,128,4]{2,3,1,0:T(4,128)S(1)} %copy.98), channel_id=1, replica_groups=mesh['wide_0'=4,'wide_1'=4,'wide_2'=2,'narrow'=4] {'wide_0','wide_1','wi..., dimensions={0} | all-to-all | bytes 2097152 | tf_op jit(solution)/shard_map/all_to_all | solution.py:205
  426.2 7.5 %multiply_reduce_fusion.1 = (f32[]{:T(128)}, f32[4,128,512]{2,1,0:T(8,128)}) fusion(f32[4,128,512]{2,1,0:T(8,128)S(1)} %copy-done.21, f32[4,128,512]{1,2,0:T(8,128)S(1)} %bitcast.219, s32[512]{0:T(512)S(1)} %multiply_add_fusion.3, f32[512]{0:T(512)S(1)} %fusion.261), kind=kOutput, calls=%fused_computation.214 | convolution fusion | flops 1615069184 | bytes 3149828 | tf_op jit(solution)/shard_map/zyk,kx->zyx/dot_general | solution.py:206
  433.7 9.5 %psum.184 = f32[]{:T(128)} all-reduce(f32[]{:T(128)} %get-tuple-element.53), channel_id=1, replica_groups=mesh['wide_0'=4,'wide_1'=4,'wide_2'=2,'narrow'=4] {'wide_0'}, use_global_device_ids=true, to_apply=%region_21.22 | all-reduce | flops 1 | bytes 8 | tf_op jit(solution)/shard_map/psum | solution.py:43
  443.2 9.6 %psum.185 = f32[]{:T(128)} all-reduce(f32[]{:T(128)} %psum.184), channel_id=1, replica_groups=mesh['wide_0'=4,'wide_1'=4,'wide_2'=2,'narrow'=4] {'wide_1'}, use_global_device_ids=true, to_apply=%region_22.23 | all-reduce | flops 1 | bytes 8 | tf_op jit(solution)/shard_map/psum | solution.py:43
  452.8 3.1 psum.186
  456.0 9.8 %psum.187 = f32[]{:T(128)} all-reduce(f32[]{:T(128)} %psum.186), channel_id=1, replica_groups=mesh['wide_0'=4,'wide_1'=4,'wide_2'=2,'narrow'=4] {'narrow'}, use_global_device_ids=true, to_apply=%region_24.25 | all-reduce | flops 1 | bytes 8 | tf_op jit(solution)/shard_map/psum | solution.py:43
  470.9 3.6 collective-permute-start.12
  476.9 3.5 collective-permute-start.14
  486.4 9.3 %psum.188 = f32[]{:T(128)} all-reduce(f32[]{:T(128)} %get-tuple-element.13), channel_id=1, replica_groups=mesh['wide_0'=4,'wide_1'=4,'wide_2'=2,'narrow'=4] {'wide_0'}, use_global_device_ids=true, to_apply=%region_26.27 | all-reduce | flops 1 | bytes 8 | tf_op jit(solution)/shard_map/psum | solution.py:43
  495.6 10.9 %psum.189 = f32[]{:T(128)} all-reduce(f32[]{:T(128)} %psum.188), channel_id=1, replica_groups=mesh['wide_0'=4,'wide_1'=4,'wide_2'=2,'narrow'=4] {'wide_1'}, use_global_device_ids=true, to_apply=%region_27.28 | all-reduce | flops 1 | bytes 8 | tf_op jit(solution)/shard_map/psum | solution.py:43
  509.6 10.3 %psum.191 = f32[]{:T(128)} all-reduce(f32[]{:T(128)} %psum.190), channel_id=1, replica_groups=mesh['wide_0'=4,'wide_1'=4,'wide_2'=2,'narrow'=4] {'narrow'}, use_global_device_ids=true, to_apply=%region_29.30 | all-reduce | flops 1 | bytes 8 | tf_op jit(solution)/shard_map/psum | solution.py:43
  521.1 3.5 multiply_subtract_fusion
  (151 shorter events, 88.1 us)
Async XLA Ops:
  0.6 37.9 %copy-start = (f32[128,128]{1,0:T(8,128)S(1)}, f32[128,128]{1,0:T(8,128)}, u32[]{:S(2)}) copy-start(f32[128,128]{1,0:T(8,128)} %param.9) | copy-start | bytes 196612
  0.6 1.6 copy-start.4
  2.2 12.5 %copy-start.23 = (s32[1,1,16]{2,1,0:T(1,128)S(1)}, s32[1,1,16]{2,1,0:T(1,128)}, u32[]{:S(2)}) copy-start(s32[1,1,16]{2,1,0:T(1,128)} %param.7) | copy-start | bytes 196
  2.3 12.8 %collective-permute-start = (f32[2,4,1,512]{3,2,1,0:T(1,128)S(1)}, f32[2,4,1,512]{3,2,1,0:T(1,128)S(1)}, u32[]{:S(2)}, u32[]{:S(2)}) collective-permute-start(f32[2,4,1,512]{3,2,1,0:T(1,128)S(1)} %get-tuple-element.30), channel_id=1, source_target_pairs={{0,1},{1,2},{2,3},{4,5},{5,6},{6,7},{8,9},{9,10},{10,11},{12,13},{... | collective-permute-start | bytes 49160 | tf_op jit(solution)/shard_map/ppermute | solution.py:29
  5.7 9.4 %collective-permute-start.3 = (f32[2,4,1,512]{3,2,1,0:T(1,128)S(1)}, f32[2,4,1,512]{3,2,1,0:T(1,128)S(1)}, u32[]{:S(2)}, u32[]{:S(2)}) collective-permute-start(f32[2,4,1,512]{3,2,1,0:T(1,128)S(1)} %get-tuple-element.31), channel_id=1, source_target_pairs={{1,0},{2,1},{3,2},{5,4},{6,5},{7,6},{9,8},{10,9},{11,10},{13,12},{... | collective-permute-start | bytes 49160 | tf_op jit(solution)/shard_map/ppermute | solution.py:30
  9.2 10.8 %collective-permute-start.1 = (f32[2,1,128,512]{3,2,1,0:T(8,128)}, f32[2,1,128,512]{3,2,1,0:T(8,128)}, u32[]{:S(2)}, u32[]{:S(2)}) collective-permute-start(f32[2,1,128,512]{3,2,1,0:T(8,128)} %get-tuple-element.28), channel_id=1, source_target_pairs={{0,4},{4,8},{8,12},{12,16},{16,20},{20,24},{24,28},{28,32},{32,36}... | collective-permute-start | bytes 1572872 | tf_op jit(solution)/shard_map/ppermute | solution.py:29
  11.1 10.6 %collective-permute-start.2 = (f32[2,1,128,512]{3,2,1,0:T(8,128)}, f32[2,1,128,512]{3,2,1,0:T(8,128)}, u32[]{:S(2)}, u32[]{:S(2)}) collective-permute-start(f32[2,1,128,512]{3,2,1,0:T(8,128)} %get-tuple-element.29), channel_id=1, source_target_pairs={{4,0},{8,4},{12,8},{16,12},{20,16},{24,20},{28,24},{32,28},{36,32}... | collective-permute-start | bytes 1572872 | tf_op jit(solution)/shard_map/ppermute | solution.py:30
  23.6 1.7 copy-start.2
  36.0 3.2 copy-start.22
  44.3 7.0 %copy-start.17 = (f32[4,128,512]{2,1,0:T(8,128)}, f32[4,128,512]{2,1,0:T(8,128)S(1)}, u32[]{:S(2)}) copy-start(f32[4,128,512]{2,1,0:T(8,128)S(1)} %reshape.309) | copy-start | bytes 3145732
  53.9 29.9 %all-to-all-start = ((f32[1,4,128,512]{2,1,0,3:T(4,128)}), f32[1,4,128,512]{2,1,0,3:T(4,128)S(1)}, u32[]{:S(2)}, u32[]{:S(2)}) async-start(f32[1,4,128,512]{2,1,0,3:T(4,128)} %copy.65), calls=%async_computation | async-start | bytes 2097152 | tf_op jit(solution)/shard_map/all_to_all | solution.py:195
  125.0 17.4 %copy-start.3 = (f32[2,6,130,512]{3,2,1,0:T(8,128)S(1)}, f32[2,6,130,512]{3,2,1,0:T(8,128)}, u32[]{:S(2)}) copy-start(f32[2,6,130,512]{3,2,1,0:T(8,128)} %copy-done.2) | copy-start | bytes 9584644
  130.9 13.3 %collective-permute-start.5 = (f32[1,128,512]{2,1,0:T(8,128)S(1)}, f32[1,128,512]{2,1,0:T(8,128)S(1)}, u32[]{:S(2)}, u32[]{:S(2)}) collective-permute-start(f32[1,128,512]{2,1,0:T(8,128)S(1)} %get-tuple-element.47), channel_id=1, source_target_pairs={{0,4},{4,8},{8,12},{12,16},{16,20},{20,24},{24,28},{28,32},{32,36}... | collective-permute-start | bytes 786440 | tf_op jit(solution)/shard_map/ppermute | solution.py:29
  132.8 11.4 %collective-permute-start.4 = (f32[1,128,512]{2,1,0:T(8,128)S(1)}, f32[1,128,512]{2,1,0:T(8,128)S(1)}, u32[]{:S(2)}, u32[]{:S(2)}) collective-permute-start(f32[1,128,512]{2,1,0:T(8,128)S(1)} %get-tuple-element.48), channel_id=1, source_target_pairs={{4,0},{8,4},{12,8},{16,12},{20,16},{24,20},{28,24},{32,28},{36,32}... | collective-permute-start | bytes 786440 | tf_op jit(solution)/shard_map/ppermute | solution.py:30
  136.5 6.5 %collective-permute-start.7 = (f32[4,1,512]{2,1,0:T(1,128)S(1)}, f32[4,1,512]{2,1,0:T(1,128)S(1)}, u32[]{:S(2)}, u32[]{:S(2)}) collective-permute-start(f32[4,1,512]{2,1,0:T(1,128)S(1)} %get-tuple-element.49), channel_id=1, source_target_pairs={{0,1},{1,2},{2,3},{4,5},{5,6},{6,7},{8,9},{9,10},{10,11},{12,13},{... | collective-permute-start | bytes 24584 | tf_op jit(solution)/shard_map/ppermute | solution.py:29
  138.6 5.5 %collective-permute-start.6 = (f32[4,1,512]{2,1,0:T(1,128)S(1)}, f32[4,1,512]{2,1,0:T(1,128)S(1)}, u32[]{:S(2)}, u32[]{:S(2)}) collective-permute-start(f32[4,1,512]{2,1,0:T(1,128)S(1)} %get-tuple-element.50), channel_id=1, source_target_pairs={{1,0},{2,1},{3,2},{5,4},{6,5},{7,6},{9,8},{10,9},{11,10},{13,12},{... | collective-permute-start | bytes 24584 | tf_op jit(solution)/shard_map/ppermute | solution.py:30
  142.9 2.0 copy-start.18
  190.0 71.0 %copy-start.19 = (f32[4,128,512]{2,1,0:T(8,128)}, f32[4,128,512]{2,1,0:T(8,128)S(1)}, u32[]{:S(2)}) copy-start(f32[4,128,512]{2,1,0:T(8,128)S(1)} %multiply_subtract_fusion.2) | copy-start | bytes 3145732
  300.7 14.8 %copy-start.13 = (f32[4,128,512]{2,1,0:T(8,128)S(1)}, f32[4,128,512]{2,1,0:T(8,128)}, u32[]{:S(2)}) copy-start(f32[4,128,512]{2,1,0:T(8,128)} %get-tuple-element.22) | copy-start | bytes 3145732
  300.7 14.8 %copy-start.15 = (f32[4,128,512]{2,1,0:T(8,128)S(1)}, f32[4,128,512]{2,1,0:T(8,128)}, u32[]{:S(2)}) copy-start(f32[4,128,512]{2,1,0:T(8,128)} %get-tuple-element.23) | copy-start | bytes 3145732
  301.0 14.6 %copy-start.11 = (f32[4,128,512]{2,1,0:T(8,128)S(1)}, f32[4,128,512]{2,1,0:T(8,128)}, u32[]{:S(2)}) copy-start(f32[4,128,512]{2,1,0:T(8,128)} %get-tuple-element.21) | copy-start | bytes 3145732
  301.0 14.6 %copy-start.5 = (f32[4,128,512]{2,1,0:T(8,128)S(1)}, f32[4,128,512]{2,1,0:T(8,128)}, u32[]{:S(2)}) copy-start(f32[4,128,512]{2,1,0:T(8,128)} %get-tuple-element.18) | copy-start | bytes 3145732
  301.0 14.6 %copy-start.7 = (f32[4,128,512]{2,1,0:T(8,128)S(1)}, f32[4,128,512]{2,1,0:T(8,128)}, u32[]{:S(2)}) copy-start(f32[4,128,512]{2,1,0:T(8,128)} %get-tuple-element.19) | copy-start | bytes 3145732
  301.0 14.6 %copy-start.9 = (f32[4,128,512]{2,1,0:T(8,128)S(1)}, f32[4,128,512]{2,1,0:T(8,128)}, u32[]{:S(2)}) copy-start(f32[4,128,512]{2,1,0:T(8,128)} %get-tuple-element.20) | copy-start | bytes 3145732
  301.0 13.7 %collective-permute-start.9 = (f32[1,128,512]{2,1,0:T(8,128)S(1)}, f32[1,128,512]{2,1,0:T(8,128)S(1)}, u32[]{:S(2)}, u32[]{:S(2)}) collective-permute-start(f32[1,128,512]{2,1,0:T(8,128)S(1)} %get-tuple-element.43), channel_id=1, source_target_pairs={{0,4},{4,8},{8,12},{12,16},{16,20},{20,24},{24,28},{28,32},{32,36}... | collective-permute-start | bytes 786440 | tf_op jit(solution)/shard_map/ppermute | solution.py:29
  303.2 11.5 %collective-permute-start.8 = (f32[1,128,512]{2,1,0:T(8,128)S(1)}, f32[1,128,512]{2,1,0:T(8,128)S(1)}, u32[]{:S(2)}, u32[]{:S(2)}) collective-permute-start(f32[1,128,512]{2,1,0:T(8,128)S(1)} %get-tuple-element.44), channel_id=1, source_target_pairs={{4,0},{8,4},{12,8},{16,12},{20,16},{24,20},{28,24},{32,28},{36,32}... | collective-permute-start | bytes 786440 | tf_op jit(solution)/shard_map/ppermute | solution.py:30
  306.9 5.9 %collective-permute-start.11 = (f32[4,1,512]{2,1,0:T(1,128)S(1)}, f32[4,1,512]{2,1,0:T(1,128)S(1)}, u32[]{:S(2)}, u32[]{:S(2)}) collective-permute-start(f32[4,1,512]{2,1,0:T(1,128)S(1)} %get-tuple-element.45), channel_id=1, source_target_pairs={{0,1},{1,2},{2,3},{4,5},{5,6},{6,7},{8,9},{9,10},{10,11},{12,13},{... | collective-permute-start | bytes 24584 | tf_op jit(solution)/shard_map/ppermute | solution.py:29
  309.2 5.5 %collective-permute-start.10 = (f32[4,1,512]{2,1,0:T(1,128)S(1)}, f32[4,1,512]{2,1,0:T(1,128)S(1)}, u32[]{:S(2)}, u32[]{:S(2)}) collective-permute-start(f32[4,1,512]{2,1,0:T(1,128)S(1)} %get-tuple-element.46), channel_id=1, source_target_pairs={{1,0},{2,1},{3,2},{5,4},{6,5},{7,6},{9,8},{10,9},{11,10},{13,12},{... | collective-permute-start | bytes 24584 | tf_op jit(solution)/shard_map/ppermute | solution.py:30
  354.1 1.0 copy-start.20
  402.9 23.3 %copy-start.21 = (f32[4,128,512]{2,1,0:T(8,128)S(1)}, f32[4,128,512]{2,1,0:T(8,128)}, u32[]{:S(2)}) copy-start(f32[4,128,512]{2,1,0:T(8,128)} %copy-done.20) | copy-start | bytes 3145732
  467.0 16.2 %copy-start.14 = (f32[4,128,512]{2,1,0:T(8,128)S(1)}, f32[4,128,512]{2,1,0:T(8,128)}, u32[]{:S(2)}) copy-start(f32[4,128,512]{2,1,0:T(8,128)} %get-tuple-element.22) | copy-start | bytes 3145732
  467.0 16.2 %copy-start.16 = (f32[4,128,512]{2,1,0:T(8,128)S(1)}, f32[4,128,512]{2,1,0:T(8,128)}, u32[]{:S(2)}) copy-start(f32[4,128,512]{2,1,0:T(8,128)} %get-tuple-element.23) | copy-start | bytes 3145732
  468.6 14.6 %copy-start.12 = (f32[4,128,512]{2,1,0:T(8,128)S(1)}, f32[4,128,512]{2,1,0:T(8,128)}, u32[]{:S(2)}) copy-start(f32[4,128,512]{2,1,0:T(8,128)} %get-tuple-element.21) | copy-start | bytes 3145732
  468.7 14.6 %copy-start.6 = (f32[4,128,512]{2,1,0:T(8,128)S(1)}, f32[4,128,512]{2,1,0:T(8,128)}, u32[]{:S(2)}) copy-start(f32[4,128,512]{2,1,0:T(8,128)} %get-tuple-element.18) | copy-start | bytes 3145732
  468.7 14.6 %copy-start.8 = (f32[4,128,512]{2,1,0:T(8,128)S(1)}, f32[4,128,512]{2,1,0:T(8,128)}, u32[]{:S(2)}) copy-start(f32[4,128,512]{2,1,0:T(8,128)} %get-tuple-element.19) | copy-start | bytes 3145732
  468.7 14.6 %copy-start.10 = (f32[4,128,512]{2,1,0:T(8,128)S(1)}, f32[4,128,512]{2,1,0:T(8,128)}, u32[]{:S(2)}) copy-start(f32[4,128,512]{2,1,0:T(8,128)} %get-tuple-element.20) | copy-start | bytes 3145732
  468.7 13.7 %collective-permute-start.13 = (f32[1,128,512]{2,1,0:T(8,128)S(1)}, f32[1,128,512]{2,1,0:T(8,128)S(1)}, u32[]{:S(2)}, u32[]{:S(2)}) collective-permute-start(f32[1,128,512]{2,1,0:T(8,128)S(1)} %get-tuple-element.39), channel_id=1, source_target_pairs={{0,4},{4,8},{8,12},{12,16},{16,20},{20,24},{24,28},{28,32},{32,36}... | collective-permute-start | bytes 786440 | tf_op jit(solution)/shard_map/ppermute | solution.py:29
  470.9 11.5 %collective-permute-start.12 = (f32[1,128,512]{2,1,0:T(8,128)S(1)}, f32[1,128,512]{2,1,0:T(8,128)S(1)}, u32[]{:S(2)}, u32[]{:S(2)}) collective-permute-start(f32[1,128,512]{2,1,0:T(8,128)S(1)} %get-tuple-element.40), channel_id=1, source_target_pairs={{4,0},{8,4},{12,8},{16,12},{20,16},{24,20},{28,24},{32,28},{36,32}... | collective-permute-start | bytes 786440 | tf_op jit(solution)/shard_map/ppermute | solution.py:30
  474.6 5.9 %collective-permute-start.15 = (f32[4,1,512]{2,1,0:T(1,128)S(1)}, f32[4,1,512]{2,1,0:T(1,128)S(1)}, u32[]{:S(2)}, u32[]{:S(2)}) collective-permute-start(f32[4,1,512]{2,1,0:T(1,128)S(1)} %get-tuple-element.41), channel_id=1, source_target_pairs={{0,1},{1,2},{2,3},{4,5},{5,6},{6,7},{8,9},{9,10},{10,11},{12,13},{... | collective-permute-start | bytes 24584 | tf_op jit(solution)/shard_map/ppermute | solution.py:29
  476.9 5.5 %collective-permute-start.14 = (f32[4,1,512]{2,1,0:T(1,128)S(1)}, f32[4,1,512]{2,1,0:T(1,128)S(1)}, u32[]{:S(2)}, u32[]{:S(2)}) collective-permute-start(f32[4,1,512]{2,1,0:T(1,128)S(1)} %get-tuple-element.42), channel_id=1, source_target_pairs={{1,0},{2,1},{3,2},{5,4},{6,5},{7,6},{9,8},{10,9},{11,10},{13,12},{... | collective-permute-start | bytes 24584 | tf_op jit(solution)/shard_map/ppermute | solution.py:30
  521.1 3.5 copy-start.1
where the time goes:
time: 535 us; the launch traced here: 525 us
  blocking collectives  278 us (52%)
  matrix products  92.4 us (17%)
  starting transfers between devices  58.2 us (11%)
  other arithmetic  36.1 us (7%)
  waiting for transfers between devices  29.2 us (5%)
  local copies, waits for them, and re-layouts  22.7 us (4%)
  between operations  8.14 us (2%)
    psum x20, blocking collectives, over_axes(): array = lax.psum(array, axis)  165 us
    all_to_all x3, blocking collectives, precondition(): lax.all_to_all(planes, WIDE_NARROW, split_axis=0, concat_axis=3, tiled=True)  69 us
    all_to_all x2, blocking collectives, precondition(): lax.all_to_all(spectrum[None], WIDE_NARROW, split_axis=3, concat_axis=0,...  43.6 us
    ppermute x8, starting transfers between devices, padded_2(): lax.ppermute(initial, axis, [(b, a) for a, b in up])  27.8 us
    dot_general x3, matrix products, precondition(): planes = jnp.einsum('mnyk,lny->mlk', planes, table_y, precision=highest)  21.7 us
    dot_general x3, matrix products, precondition(): spectrum = jnp.einsum('zyx,kx->zyk', remainder, table_x, precision=highest)  20.5 us
    dot_general x3, matrix products, precondition(): return jnp.einsum('zyk,kx->zyx', slabs[0], table_x, precision=highest)  19.9 us
    dot_general x3, matrix products, precondition(): jnp.einsum('mlk,lny->mnyk', planes / denom, table_y, precision=highest)  18.4 us
  transfers between devices with their start and end apart: 17, of which 6 were waited for; matrix products, arithmetic and copies ran while one was open for 0% of the time, Pallas kernels for 0%

commit v1 on v0

--- a/solution.py
+++ b/solution.py
@@ -40,7 +40,8 @@
 
 def over_axes(array, axes):
     for axis in axes:
-        array = lax.psum(array, axis)
+        parts = lax.all_gather(array, axis)
+        array = jnp.sum(parts, axis=0)
     return array
 
 

time: 535 us -> 569 us (1.064)
  the two profiles are of different devices: /device:TPU:34 before, /device:TPU:0 now
where the time goes in v1:
time: 569 us; the launch traced here: 558 us
  blocking collectives  240 us (42%)
  matrix products  92.6 us (16%)
  starting transfers between devices  65.9 us (12%)
  local copies, waits for them, and re-layouts  58.8 us (10%)
  other arithmetic  51.2 us (9%)
  waiting for transfers between devices  40.9 us (7%)
  between operations  8.53 us (1%)
    unnamed x20, blocking collectives  149 us
    all_to_all x2, blocking collectives, precondition(): lax.all_to_all(planes, WIDE_NARROW, split_axis=0, concat_axis=3, tiled=True)  46.1 us
    all_to_all x2, blocking collectives, precondition(): lax.all_to_all(spectrum[None], WIDE_NARROW, split_axis=3, concat_axis=0,...  45.8 us
    unnamed x111, local copies, waits for them, and re-layouts  38.7 us
    ppermute x8, starting transfers between devices, padded_2(): lax.ppermute(last, axis, up)  31.2 us
    dot_general x3, matrix products, precondition(): planes = jnp.einsum('mnyk,lny->mlk', planes, table_y, precision=highest)  21.7 us
    dot_general x3, matrix products, precondition(): spectrum = jnp.einsum('zyx,kx->zyk', remainder, table_x, precision=highest)  20.5 us
    dot_general x3, matrix products, precondition(): return jnp.einsum('zyk,kx->zyx', slabs[0], table_x, precision=highest)  19.9 us
  transfers between devices with their start and end apart: 18, of which 6 were waited for; matrix products, arithmetic and copies ran while one was open for 1% of the time, Pallas kernels for 0%

profile of v1, /device:TPU:0, one launch (start us, length us, event | category | flops | bytes accessed | tf_op | source)
XLA Modules:
  0.0 558.4 jit_solution(16336040777913412727)
XLA Ops:
  3.6 4.5 collective-permute-start
  10.5 3.9 collective-permute-start.1
  20.9 4.9 fusion.6
  38.0 7.0 %convolution_bitcast_fusion.15 = f32[1,4,128,512]{3,2,1,0:T(8,128)} fusion(f32[4,128,512]{2,1,0:T(8,128)S(1)} %reshape.309, s32[512]{0:T(512)S(1)} %multiply_add_fusion.3, f32[512]{0:T(512)S(1)} %fusion.261), kind=kOutput, calls=%fused_computation.47 | convolution fusion | flops 1614544896 | bytes 2101248 | tf_op jit(solution)/shard_map/zyx,kx->zyk/dot_general | solution.py:195
  47.5 19.2 %all-to-all-start = ((f32[1,4,128,512]{2,1,0,3:T(4,128)}), f32[1,4,128,512]{2,1,0,3:T(4,128)S(1)}, u32[]{:S(2)}, u32[]{:S(2)}) async-start(f32[1,4,128,512]{2,1,0,3:T(4,128)} %copy.65), calls=%async_computation | async-start | bytes 2097152 | tf_op jit(solution)/shard_map/all_to_all | solution.py:196
  67.1 18.6 %all-to-all-done = f32[1,4,128,512]{2,1,0,3:T(4,128)S(1)} async-done(((f32[1,4,128,512]{2,1,0,3:T(4,128)}), f32[1,4,128,512]{2,1,0,3:T(4,128)S(1)}, u32[]{:S(2)}, u32[]{:S(2)}) %all-to-all-start) | async-done | bytes 1048608 | tf_op jit(solution)/shard_map/all_to_all | solution.py:196
  87.3 7.2 %convolution_bitcast_fusion.13 = f32[128,512,4]{0,1,2:T(8,128)S(1)} fusion(f32[128,4,128,4]{2,0,1,3:T(8,128)S(1)} %convolution_bitcast_fusion.14, s32[4,128]{1,0:T(4,128)S(1)} %multiply_add_fusion.4, f32[512]{0:T(512)S(1)} %fusion.261), kind=kOutput, calls=%fused_computation.45 | convolution fusion | flops 1614544896 | bytes 2101248 | tf_op jit(solution)/shard_map/mnyk,lny->mlk/dot_general | solution.py:201
  94.6 6.3 %convolution_bitcast_fusion.12 = f32[128,4,128,4,1]{0,2,3,1,4:T(8,128)S(1)} fusion(f32[128,512,4]{0,1,2:T(8,128)S(1)} %convolution_bitcast_fusion.13, f32[4]{0:T(128)S(1)} %multiply_multiply_fusion.1, f32[128,512]{0,1:T(8,128)S(1)} %broadcast_add_fusion, s32[4,128]{1,0:T(4,128)S(1)} %multiply_add_fusion.4, f32[512]{0:T(512)S(1)} %fusion.261), kind=kOutput, calls=%fused_computation.44 | convolution fusion | flops 1615331328 | bytes 2363408 | tf_op jit(solution)/shard_map/mlk,lny->mnyk/dot_general | solution.py:203
  104.6 4.6 all-to-all-start.1
  109.8 18.3 %all-to-all-done.1 = f32[128,4,128,4]{2,3,1,0:T(4,128)S(1)} async-done(((f32[128,4,128,4]{2,3,1,0:T(4,128)}), f32[128,4,128,4]{2,3,1,0:T(4,128)S(1)}, u32[]{:S(2)}, u32[]{:S(2)}) %all-to-all-start.1) | async-done | bytes 1048608 | tf_op jit(solution)/shard_map/all_to_all | solution.py:206
  128.3 5.8 %fusion.126 = f32[4,128,512]{2,1,0:T(8,128)S(1)} fusion(f32[4,128,512]{1,2,0:T(8,128)S(1)} %bitcast.249, s32[512]{0:T(512)S(1)} %multiply_add_fusion.3, f32[512]{0:T(512)S(1)} %fusion.261), kind=kOutput, calls=%fused_computation.235 | convolution fusion | flops 1614544896 | bytes 2101248 | tf_op jit(solution)/shard_map/zyk,kx->zyx/dot_general | solution.py:207
  135.5 3.0 collective-permute-start.5
  139.9 4.5 collective-permute-start.7
  146.6 7.6 %multiply_reduce_fusion.4 = (f32[]{:T(128)}, f32[]{:T(128)}, f32[4,128,512]{2,1,0:T(8,128)}, f32[4,128,512]{2,1,0:T(8,128)}, f32[4,128,512]{2,1,0:T(8,128)}, /*i...) fusion(f32[4,128,512]{2,1,0:T(8,128)S(1)} %fusion.126, ...), kind=kLoop, calls=%fused_computation.222 | loop fusion | flops 12845054 | bytes 25714696 | tf_op jit(solution)/shard_map/reduce_sum | solution.py:217
  157.5 9.7 %all-reduce.38 = (f32[4]{0:T(128)S(1)}, f32[4]{0:T(128)S(1)}) all-reduce(f32[4]{0:T(128)S(1)} %dynamic-update-slice, f32[4]{0:T(128)S(1)} %dynamic-update-slice.4), channel_id=1, replica_groups=mesh['wide_0'=4,'wide_1'=4,'wide_2'=2,'narrow'=4] {'wide_0'}, use_global_device_ids=true, to_apply=%add.12 | all-reduce | flops 8 | bytes 64
  171.8 8.2 %all-reduce.37 = (f32[4]{0:T(128)S(1)}, f32[4]{0:T(128)S(1)}) all-reduce(f32[4]{0:T(128)S(1)} %dynamic-update-slice.1, f32[4]{0:T(128)S(1)} %dynamic-update-slice.5), channel_id=1, replica_groups=mesh['wide_0'=4,'wide_1'=4,'wide_2'=2,'narrow'=4] {'wide_1'}, use_global_device_ids=true, to_apply=%add.13 | all-reduce | flops 8 | bytes 64
  184.6 2.6 all-reduce.39
  191.2 10.0 %all-reduce.36 = (f32[4]{0:T(128)S(1)}, f32[4]{0:T(128)S(1)}) all-reduce(f32[4]{0:T(128)S(1)} %dynamic-update-slice.3, f32[4]{0:T(128)S(1)} %dynamic-update-slice.7), channel_id=1, replica_groups=mesh['wide_0'=4,'wide_1'=4,'wide_2'=2,'narrow'=4] {'narrow'}, use_global_device_ids=true, to_apply=%add.15 | all-reduce | flops 8 | bytes 64
  205.6 6.8 %convolution_bitcast_fusion.10 = f32[1,4,128,512]{3,2,1,0:T(8,128)} fusion(f32[4,128,512]{2,1,0:T(8,128)S(1)} %multiply_subtract_fusion.2, s32[512]{0:T(512)S(1)} %multiply_add_fusion.3, f32[512]{0:T(512)S(1)} %fusion.261), kind=kOutput, calls=%fused_computation.42 | convolution fusion | flops 1614544896 | bytes 2101248 | tf_op jit(solution)/shard_map/zyx,kx->zyk/dot_general | solution.py:195
  214.0 22.9 %all_to_all.90 = f32[1,4,128,512]{2,1,0,3:T(4,128)S(1)} all-to-all(f32[1,4,128,512]{2,1,0,3:T(4,128)S(1)} %copy.77), channel_id=1, replica_groups=mesh['wide_0'=4,'wide_1'=4,'wide_2'=2,'narrow'=4] {'wide_0','wide_1','wi..., dimensions={3} | all-to-all | bytes 2097152 | tf_op jit(solution)/shard_map/all_to_all | solution.py:196
  238.5 7.2 %convolution_bitcast_fusion.8 = f32[128,512,4]{0,1,2:T(8,128)S(1)} fusion(f32[128,4,128,4]{2,0,1,3:T(8,128)S(1)} %convolution_bitcast_fusion.9, s32[4,128]{1,0:T(4,128)S(1)} %multiply_add_fusion.4, f32[512]{0:T(512)S(1)} %fusion.261), kind=kOutput, calls=%fused_computation.40 | convolution fusion | flops 1614544896 | bytes 2101248 | tf_op jit(solution)/shard_map/mnyk,lny->mlk/dot_general | solution.py:201
  245.8 6.3 %convolution_bitcast_fusion.7 = f32[128,4,128,4,1]{0,2,3,1,4:T(8,128)S(1)} fusion(f32[128,512,4]{0,1,2:T(8,128)S(1)} %convolution_bitcast_fusion.8, f32[4]{0:T(128)S(1)} %multiply_multiply_fusion.1, f32[128,512]{0,1:T(8,128)S(1)} %broadcast_add_fusion, s32[4,128]{1,0:T(4,128)S(1)} %multiply_add_fusion.4, f32[512]{0:T(512)S(1)} %fusion.261), kind=kOutput, calls=%fused_computation.39 | convolution fusion | flops 1615331328 | bytes 2363408 | tf_op jit(solution)/shard_map/mlk,lny->mnyk/dot_general | solution.py:203
  254.8 23.1 %all_to_all.91 = f32[128,4,128,4]{2,3,1,0:T(4,128)S(1)} all-to-all(f32[128,4,128,4]{2,3,1,0:T(4,128)S(1)} %copy.86), channel_id=1, replica_groups=mesh['wide_0'=4,'wide_1'=4,'wide_2'=2,'narrow'=4] {'wide_0','wide_1','wi..., dimensions={0} | all-to-all | bytes 2097152 | tf_op jit(solution)/shard_map/all_to_all | solution.py:206
  278.1 6.6 %multiply_reduce_fusion.3 = (f32[]{:T(128)}, f32[4,128,512]{2,1,0:T(8,128)S(1)}) fusion(f32[4,128,512]{2,1,0:T(8,128)S(1)} %multiply_subtract_fusion.2, f32[4,128,512]{1,2,0:T(8,128)S(1)} %bitcast.248, s32[512]{0:T(512)S(1)} %multiply_add_fusion.3, f32[512]{0:T(512)S(1)} %fusion.261), kind=kOutput, calls=%fused_computation.219 | convolution fusion | flops 1615069184 | bytes 3149828 | tf_op jit(solution)/shard_map/zyk,kx->zyx/dot_general | solution.py:207
  286.0 8.8 %all-reduce.20 = f32[4]{0:T(128)S(1)} all-reduce(f32[4]{0:T(128)S(1)} %dynamic-update-slice.8), channel_id=1, replica_groups=mesh['wide_0'=4,'wide_1'=4,'wide_2'=2,'narrow'=4] {'wide_0'}, use_global_device_ids=true, to_apply=%add.20 | all-reduce | flops 4 | bytes 32
  296.8 8.5 %all-reduce.21 = f32[4]{0:T(128)S(1)} all-reduce(f32[4]{0:T(128)S(1)} %dynamic-update-slice.9), channel_id=1, replica_groups=mesh['wide_0'=4,'wide_1'=4,'wide_2'=2,'narrow'=4] {'wide_1'}, use_global_device_ids=true, to_apply=%add.21 | all-reduce | flops 4 | bytes 32
  311.7 8.5 %all-reduce.23 = f32[4]{0:T(128)S(1)} all-reduce(f32[4]{0:T(128)S(1)} %dynamic-update-slice.11), channel_id=1, replica_groups=mesh['wide_0'=4,'wide_1'=4,'wide_2'=2,'narrow'=4] {'narrow'}, use_global_device_ids=true, to_apply=%add.23 | all-reduce | flops 4 | bytes 32
  324.1 3.0 collective-permute-start.9
  328.5 4.5 collective-permute-start.11
  338.8 9.1 %all-reduce.24 = f32[4]{0:T(128)S(1)} all-reduce(f32[4]{0:T(128)S(1)} %dynamic-update-slice.12), channel_id=1, replica_groups=mesh['wide_0'=4,'wide_1'=4,'wide_2'=2,'narrow'=4] {'wide_0'}, use_global_device_ids=true, to_apply=%add.24 | all-reduce | flops 4 | bytes 32
  349.9 9.2 %all-reduce.25 = f32[4]{0:T(128)S(1)} all-reduce(f32[4]{0:T(128)S(1)} %dynamic-update-slice.13), channel_id=1, replica_groups=mesh['wide_0'=4,'wide_1'=4,'wide_2'=2,'narrow'=4] {'wide_1'}, use_global_device_ids=true, to_apply=%add.25 | all-reduce | flops 4 | bytes 32
  365.5 10.0 %all-reduce.27 = f32[4]{0:T(128)S(1)} all-reduce(f32[4]{0:T(128)S(1)} %dynamic-update-slice.15), channel_id=1, replica_groups=mesh['wide_0'=4,'wide_1'=4,'wide_2'=2,'narrow'=4] {'narrow'}, use_global_device_ids=true, to_apply=%add.27 | all-reduce | flops 4 | bytes 32
  379.9 6.8 %convolution_bitcast_fusion.5 = f32[1,4,128,512]{3,2,1,0:T(8,128)} fusion(f32[4,128,512]{2,1,0:T(8,128)S(1)} %multiply_subtract_fusion.1, s32[512]{0:T(512)S(1)} %multiply_add_fusion.3, f32[512]{0:T(512)S(1)} %fusion.261), kind=kOutput, calls=%fused_computation.37 | convolution fusion | flops 1614544896 | bytes 2101248 | tf_op jit(solution)/shard_map/zyx,kx->zyk/dot_general | solution.py:195
  388.3 22.9 %all_to_all.92 = f32[1,4,128,512]{2,1,0,3:T(4,128)S(1)} all-to-all(f32[1,4,128,512]{2,1,0,3:T(4,128)S(1)} %copy.89), channel_id=1, replica_groups=mesh['wide_0'=4,'wide_1'=4,'wide_2'=2,'narrow'=4] {'wide_0','wide_1','wi..., dimensions={3} | all-to-all | bytes 2097152 | tf_op jit(solution)/shard_map/all_to_all | solution.py:196
  412.9 7.2 %convolution_bitcast_fusion.3 = f32[128,512,4]{0,1,2:T(8,128)S(1)} fusion(f32[128,4,128,4]{2,0,1,3:T(8,128)S(1)} %convolution_bitcast_fusion.4, s32[4,128]{1,0:T(4,128)S(1)} %multiply_add_fusion.4, f32[512]{0:T(512)S(1)} %fusion.261), kind=kOutput, calls=%fused_computation.35 | convolution fusion | flops 1614544896 | bytes 2101248 | tf_op jit(solution)/shard_map/mnyk,lny->mlk/dot_general | solution.py:201
  420.1 6.0 %convolution_bitcast_fusion.2 = f32[128,4,128,4,1]{0,2,3,1,4:T(8,128)S(1)} fusion(f32[128,512,4]{0,1,2:T(8,128)S(1)} %convolution_bitcast_fusion.3, f32[4]{0:T(128)S(1)} %multiply_multiply_fusion.1, f32[128,512]{0,1:T(8,128)S(1)} %broadcast_add_fusion, s32[4,128]{1,0:T(4,128)S(1)} %multiply_add_fusion.4, f32[512]{0:T(512)S(1)} %fusion.261), kind=kOutput, calls=%fused_computation.34 | convolution fusion | flops 1615331328 | bytes 2363408 | tf_op jit(solution)/shard_map/mlk,lny->mnyk/dot_general | solution.py:203
  428.9 23.0 %all_to_all.93 = f32[128,4,128,4]{2,3,1,0:T(4,128)S(1)} all-to-all(f32[128,4,128,4]{2,3,1,0:T(4,128)S(1)} %copy.98), channel_id=1, replica_groups=mesh['wide_0'=4,'wide_1'=4,'wide_2'=2,'narrow'=4] {'wide_0','wide_1','wi..., dimensions={0} | all-to-all | bytes 2097152 | tf_op jit(solution)/shard_map/all_to_all | solution.py:206
  452.2 7.5 %multiply_reduce_fusion.1 = (f32[]{:T(128)}, f32[4,128,512]{2,1,0:T(8,128)}) fusion(f32[4,128,512]{2,1,0:T(8,128)S(1)} %copy-done.21, f32[4,128,512]{1,2,0:T(8,128)S(1)} %bitcast.247, s32[512]{0:T(512)S(1)} %multiply_add_fusion.3, f32[512]{0:T(512)S(1)} %fusion.261), kind=kOutput, calls=%fused_computation.214 | convolution fusion | flops 1615069184 | bytes 3149828 | tf_op jit(solution)/shard_map/zyk,kx->zyx/dot_general | solution.py:207
  460.9 8.8 %all-reduce.28 = f32[4]{0:T(128)S(1)} all-reduce(f32[4]{0:T(128)S(1)} %dynamic-update-slice.16), channel_id=1, replica_groups=mesh['wide_0'=4,'wide_1'=4,'wide_2'=2,'narrow'=4] {'wide_0'}, use_global_device_ids=true, to_apply=%add.28 | all-reduce | flops 4 | bytes 32
  471.6 8.5 %all-reduce.29 = f32[4]{0:T(128)S(1)} all-reduce(f32[4]{0:T(128)S(1)} %dynamic-update-slice.17), channel_id=1, replica_groups=mesh['wide_0'=4,'wide_1'=4,'wide_2'=2,'narrow'=4] {'wide_1'}, use_global_device_ids=true, to_apply=%add.29 | all-reduce | flops 4 | bytes 32
  486.4 8.5 %all-reduce.31 = f32[4]{0:T(128)S(1)} all-reduce(f32[4]{0:T(128)S(1)} %dynamic-update-slice.19), channel_id=1, replica_groups=mesh['wide_0'=4,'wide_1'=4,'wide_2'=2,'narrow'=4] {'narrow'}, use_global_device_ids=true, to_apply=%add.31 | all-reduce | flops 4 | bytes 32
  500.1 3.0 collective-permute-start.13
  504.4 4.5 collective-permute-start.15
  511.2 3.1 multiply_reduce_fusion
  515.6 9.1 %all-reduce.32 = f32[4]{0:T(128)S(1)} all-reduce(f32[4]{0:T(128)S(1)} %dynamic-update-slice.20), channel_id=1, replica_groups=mesh['wide_0'=4,'wide_1'=4,'wide_2'=2,'narrow'=4] {'wide_0'}, use_global_device_ids=true, to_apply=%add.32 | all-reduce | flops 4 | bytes 32
  526.8 9.2 %all-reduce.33 = f32[4]{0:T(128)S(1)} all-reduce(f32[4]{0:T(128)S(1)} %dynamic-update-slice.21), channel_id=1, replica_groups=mesh['wide_0'=4,'wide_1'=4,'wide_2'=2,'narrow'=4] {'wide_1'}, use_global_device_ids=true, to_apply=%add.33 | all-reduce | flops 4 | bytes 32
  542.7 10.0 %all-reduce.35 = f32[4]{0:T(128)S(1)} all-reduce(f32[4]{0:T(128)S(1)} %dynamic-update-slice.23), channel_id=1, replica_groups=mesh['wide_0'=4,'wide_1'=4,'wide_2'=2,'narrow'=4] {'narrow'}, use_global_device_ids=true, to_apply=%add.35 | all-reduce | flops 4 | bytes 32
  554.7 3.5 multiply_subtract_fusion
  (236 shorter events, 127.4 us)
Async XLA Ops:
  0.6 31.5 %copy-start = (f32[128,128]{1,0:T(8,128)S(1)}, f32[128,128]{1,0:T(8,128)}, u32[]{:S(2)}) copy-start(f32[128,128]{1,0:T(8,128)} %param.9) | copy-start | bytes 196612
  0.6 1.6 copy-start.4
  2.2 12.1 %copy-start.23 = (s32[1,1,16]{2,1,0:T(1,128)S(1)}, s32[1,1,16]{2,1,0:T(1,128)}, u32[]{:S(2)}) copy-start(s32[1,1,16]{2,1,0:T(1,128)} %param.7) | copy-start | bytes 196
  2.3 12.4 %collective-permute-start.3 = (f32[2,4,1,512]{3,2,1,0:T(1,128)S(1)}, f32[2,4,1,512]{3,2,1,0:T(1,128)S(1)}, u32[]{:S(2)}, u32[]{:S(2)}) collective-permute-start(f32[2,4,1,512]{3,2,1,0:T(1,128)S(1)} %get-tuple-element.31), channel_id=1, source_target_pairs={{1,0},{2,1},{3,2},{5,4},{6,5},{7,6},{9,8},{10,9},{11,10},{13,12},{... | collective-permute-start | bytes 49160 | tf_op jit(solution)/shard_map/ppermute | solution.py:30
  3.6 11.1 %collective-permute-start = (f32[2,4,1,512]{3,2,1,0:T(1,128)S(1)}, f32[2,4,1,512]{3,2,1,0:T(1,128)S(1)}, u32[]{:S(2)}, u32[]{:S(2)}) collective-permute-start(f32[2,4,1,512]{3,2,1,0:T(1,128)S(1)} %get-tuple-element.30), channel_id=1, source_target_pairs={{0,1},{1,2},{2,3},{4,5},{5,6},{6,7},{8,9},{9,10},{10,11},{12,13},{... | collective-permute-start | bytes 49160 | tf_op jit(solution)/shard_map/ppermute | solution.py:29
  9.2 5.5 collective-permute-start.2
  10.5 4.9 collective-permute-start.1
  17.2 1.7 copy-start.2
  29.6 3.2 copy-start.22
  38.0 7.0 %copy-start.17 = (f32[4,128,512]{2,1,0:T(8,128)}, f32[4,128,512]{2,1,0:T(8,128)S(1)}, u32[]{:S(2)}) copy-start(f32[4,128,512]{2,1,0:T(8,128)S(1)} %reshape.309) | copy-start | bytes 3145732
  47.5 38.1 %all-to-all-start = ((f32[1,4,128,512]{2,1,0,3:T(4,128)}), f32[1,4,128,512]{2,1,0,3:T(4,128)S(1)}, u32[]{:S(2)}, u32[]{:S(2)}) async-start(f32[1,4,128,512]{2,1,0,3:T(4,128)} %copy.65), calls=%async_computation | async-start | bytes 2097152 | tf_op jit(solution)/shard_map/all_to_all | solution.py:196
  102.9 6.3 %copy-start.27 = (u32[128]{0:T(128)S(1)}, u32[128]{0:T(128)}, u32[]{:S(2)}) copy-start(u32[128]{0:T(128)} %constant.153) | copy-start | bytes 1540
  104.6 23.6 %all-to-all-start.1 = ((f32[128,4,128,4]{2,3,1,0:T(4,128)}), f32[128,4,128,4]{2,3,1,0:T(4,128)S(1)}, u32[]{:S(2)}, u32[]{:S(2)}) async-start(f32[128,4,128,4]{2,3,1,0:T(4,128)} %copy.74), calls=%async_computation.1 | async-start | bytes 2097152 | tf_op jit(solution)/shard_map/all_to_all | solution.py:206
  128.3 16.1 %copy-start.3 = (f32[2,6,130,512]{3,2,1,0:T(8,128)S(1)}, f32[2,6,130,512]{3,2,1,0:T(8,128)}, u32[]{:S(2)}) copy-start(f32[2,6,130,512]{3,2,1,0:T(8,128)} %copy-done.2) | copy-start | bytes 9584644
  134.2 11.6 %collective-permute-start.4 = (f32[1,128,512]{2,1,0:T(8,128)S(1)}, f32[1,128,512]{2,1,0:T(8,128)S(1)}, u32[]{:S(2)}, u32[]{:S(2)}) collective-permute-start(f32[1,128,512]{2,1,0:T(8,128)S(1)} %get-tuple-element.48), channel_id=1, source_target_pairs={{4,0},{8,4},{12,8},{16,12},{20,16},{24,20},{28,24},{32,28},{36,32}... | collective-permute-start | bytes 786440 | tf_op jit(solution)/shard_map/ppermute | solution.py:30
  135.5 10.3 %collective-permute-start.5 = (f32[1,128,512]{2,1,0:T(8,128)S(1)}, f32[1,128,512]{2,1,0:T(8,128)S(1)}, u32[]{:S(2)}, u32[]{:S(2)}) collective-permute-start(f32[1,128,512]{2,1,0:T(8,128)S(1)} %get-tuple-element.47), channel_id=1, source_target_pairs={{0,4},{4,8},{8,12},{12,16},{16,20},{20,24},{24,28},{28,32},{32,36}... | collective-permute-start | bytes 786440 | tf_op jit(solution)/shard_map/ppermute | solution.py:29
  138.6 6.5 %collective-permute-start.6 = (f32[4,1,512]{2,1,0:T(1,128)S(1)}, f32[4,1,512]{2,1,0:T(1,128)S(1)}, u32[]{:S(2)}, u32[]{:S(2)}) collective-permute-start(f32[4,1,512]{2,1,0:T(1,128)S(1)} %get-tuple-element.50), channel_id=1, source_target_pairs={{1,0},{2,1},{3,2},{5,4},{6,5},{7,6},{9,8},{10,9},{11,10},{13,12},{... | collective-permute-start | bytes 24584 | tf_op jit(solution)/shard_map/ppermute | solution.py:30
  139.9 5.9 %collective-permute-start.7 = (f32[4,1,512]{2,1,0:T(1,128)S(1)}, f32[4,1,512]{2,1,0:T(1,128)S(1)}, u32[]{:S(2)}, u32[]{:S(2)}) collective-permute-start(f32[4,1,512]{2,1,0:T(1,128)S(1)} %get-tuple-element.49), channel_id=1, source_target_pairs={{0,1},{1,2},{2,3},{4,5},{5,6},{6,7},{8,9},{9,10},{10,11},{12,13},{... | collective-permute-start | bytes 24584 | tf_op jit(solution)/shard_map/ppermute | solution.py:29
  145.1 1.5 copy-start.18
  146.6 10.3 %copy-start.26 = (u32[128]{0:T(128)S(1)}, u32[128]{0:T(128)}, u32[]{:S(2)}) copy-start(u32[128]{0:T(128)} %constant.158) | copy-start | bytes 1540
  146.6 24.6 %copy-start.25 = (u32[128]{0:T(128)S(1)}, u32[128]{0:T(128)}, u32[]{:S(2)}) copy-start(u32[128]{0:T(128)} %constant.163) | copy-start | bytes 1540
  146.6 37.4 %copy-start.24 = (u32[128]{0:T(128)S(1)}, u32[128]{0:T(128)}, u32[]{:S(2)}) copy-start(u32[128]{0:T(128)} %constant.168) | copy-start | bytes 1540
  205.6 72.5 %copy-start.19 = (f32[4,128,512]{2,1,0:T(8,128)}, f32[4,128,512]{2,1,0:T(8,128)S(1)}, u32[]{:S(2)}) copy-start(f32[4,128,512]{2,1,0:T(8,128)S(1)} %multiply_subtract_fusion.2) | copy-start | bytes 3145732
  322.2 13.0 %copy-start.13 = (f32[4,128,512]{2,1,0:T(8,128)S(1)}, f32[4,128,512]{2,1,0:T(8,128)}, u32[]{:S(2)}) copy-start(f32[4,128,512]{2,1,0:T(8,128)} %get-tuple-element.22) | copy-start | bytes 3145732
  322.3 13.0 %copy-start.15 = (f32[4,128,512]{2,1,0:T(8,128)S(1)}, f32[4,128,512]{2,1,0:T(8,128)}, u32[]{:S(2)}) copy-start(f32[4,128,512]{2,1,0:T(8,128)} %get-tuple-element.23) | copy-start | bytes 3145732
  322.5 12.7 %copy-start.11 = (f32[4,128,512]{2,1,0:T(8,128)S(1)}, f32[4,128,512]{2,1,0:T(8,128)}, u32[]{:S(2)}) copy-start(f32[4,128,512]{2,1,0:T(8,128)} %get-tuple-element.21) | copy-start | bytes 3145732
  322.6 12.7 %copy-start.5 = (f32[4,128,512]{2,1,0:T(8,128)S(1)}, f32[4,128,512]{2,1,0:T(8,128)}, u32[]{:S(2)}) copy-start(f32[4,128,512]{2,1,0:T(8,128)} %get-tuple-element.18) | copy-start | bytes 3145732
  322.6 12.7 %copy-start.7 = (f32[4,128,512]{2,1,0:T(8,128)S(1)}, f32[4,128,512]{2,1,0:T(8,128)}, u32[]{:S(2)}) copy-start(f32[4,128,512]{2,1,0:T(8,128)} %get-tuple-element.19) | copy-start | bytes 3145732
  322.6 12.7 %copy-start.9 = (f32[4,128,512]{2,1,0:T(8,128)S(1)}, f32[4,128,512]{2,1,0:T(8,128)}, u32[]{:S(2)}) copy-start(f32[4,128,512]{2,1,0:T(8,128)} %get-tuple-element.20) | copy-start | bytes 3145732
  322.6 11.9 %collective-permute-start.8 = (f32[1,128,512]{2,1,0:T(8,128)S(1)}, f32[1,128,512]{2,1,0:T(8,128)S(1)}, u32[]{:S(2)}, u32[]{:S(2)}) collective-permute-start(f32[1,128,512]{2,1,0:T(8,128)S(1)} %get-tuple-element.44), channel_id=1, source_target_pairs={{4,0},{8,4},{12,8},{16,12},{20,16},{24,20},{28,24},{32,28},{36,32}... | collective-permute-start | bytes 786440 | tf_op jit(solution)/shard_map/ppermute | solution.py:30
  324.1 10.3 %collective-permute-start.9 = (f32[1,128,512]{2,1,0:T(8,128)S(1)}, f32[1,128,512]{2,1,0:T(8,128)S(1)}, u32[]{:S(2)}, u32[]{:S(2)}) collective-permute-start(f32[1,128,512]{2,1,0:T(8,128)S(1)} %get-tuple-element.43), channel_id=1, source_target_pairs={{0,4},{4,8},{8,12},{12,16},{16,20},{20,24},{24,28},{28,32},{32,36}... | collective-permute-start | bytes 786440 | tf_op jit(solution)/shard_map/ppermute | solution.py:29
  327.2 5.9 %collective-permute-start.10 = (f32[4,1,512]{2,1,0:T(1,128)S(1)}, f32[4,1,512]{2,1,0:T(1,128)S(1)}, u32[]{:S(2)}, u32[]{:S(2)}) collective-permute-start(f32[4,1,512]{2,1,0:T(1,128)S(1)} %get-tuple-element.46), channel_id=1, source_target_pairs={{1,0},{2,1},{3,2},{5,4},{6,5},{7,6},{9,8},{10,9},{11,10},{13,12},{... | collective-permute-start | bytes 24584 | tf_op jit(solution)/shard_map/ppermute | solution.py:30
  328.5 5.9 %collective-permute-start.11 = (f32[4,1,512]{2,1,0:T(1,128)S(1)}, f32[4,1,512]{2,1,0:T(1,128)S(1)}, u32[]{:S(2)}, u32[]{:S(2)}) collective-permute-start(f32[4,1,512]{2,1,0:T(1,128)S(1)} %get-tuple-element.45), channel_id=1, source_target_pairs={{0,1},{1,2},{2,3},{4,5},{5,6},{6,7},{8,9},{9,10},{10,11},{12,13},{... | collective-permute-start | bytes 24584 | tf_op jit(solution)/shard_map/ppermute | solution.py:29
  379.0 1.0 copy-start.20
  428.9 23.2 %copy-start.21 = (f32[4,128,512]{2,1,0:T(8,128)S(1)}, f32[4,128,512]{2,1,0:T(8,128)}, u32[]{:S(2)}) copy-start(f32[4,128,512]{2,1,0:T(8,128)} %copy-done.20) | copy-start | bytes 3145732
  496.8 14.3 %copy-start.14 = (f32[4,128,512]{2,1,0:T(8,128)S(1)}, f32[4,128,512]{2,1,0:T(8,128)}, u32[]{:S(2)}) copy-start(f32[4,128,512]{2,1,0:T(8,128)} %get-tuple-element.22) | copy-start | bytes 3145732
  496.8 14.3 %copy-start.16 = (f32[4,128,512]{2,1,0:T(8,128)S(1)}, f32[4,128,512]{2,1,0:T(8,128)}, u32[]{:S(2)}) copy-start(f32[4,128,512]{2,1,0:T(8,128)} %get-tuple-element.23) | copy-start | bytes 3145732
  498.4 12.7 %copy-start.12 = (f32[4,128,512]{2,1,0:T(8,128)S(1)}, f32[4,128,512]{2,1,0:T(8,128)}, u32[]{:S(2)}) copy-start(f32[4,128,512]{2,1,0:T(8,128)} %get-tuple-element.21) | copy-start | bytes 3145732
  498.5 12.7 %copy-start.6 = (f32[4,128,512]{2,1,0:T(8,128)S(1)}, f32[4,128,512]{2,1,0:T(8,128)}, u32[]{:S(2)}) copy-start(f32[4,128,512]{2,1,0:T(8,128)} %get-tuple-element.18) | copy-start | bytes 3145732
  498.5 12.7 %copy-start.8 = (f32[4,128,512]{2,1,0:T(8,128)S(1)}, f32[4,128,512]{2,1,0:T(8,128)}, u32[]{:S(2)}) copy-start(f32[4,128,512]{2,1,0:T(8,128)} %get-tuple-element.19) | copy-start | bytes 3145732
  498.5 12.7 %copy-start.10 = (f32[4,128,512]{2,1,0:T(8,128)S(1)}, f32[4,128,512]{2,1,0:T(8,128)}, u32[]{:S(2)}) copy-start(f32[4,128,512]{2,1,0:T(8,128)} %get-tuple-element.20) | copy-start | bytes 3145732
  498.5 11.9 %collective-permute-start.12 = (f32[1,128,512]{2,1,0:T(8,128)S(1)}, f32[1,128,512]{2,1,0:T(8,128)S(1)}, u32[]{:S(2)}, u32[]{:S(2)}) collective-permute-start(f32[1,128,512]{2,1,0:T(8,128)S(1)} %get-tuple-element.40), channel_id=1, source_target_pairs={{4,0},{8,4},{12,8},{16,12},{20,16},{24,20},{28,24},{32,28},{36,32}... | collective-permute-start | bytes 786440 | tf_op jit(solution)/shard_map/ppermute | solution.py:30
  500.1 10.3 %collective-permute-start.13 = (f32[1,128,512]{2,1,0:T(8,128)S(1)}, f32[1,128,512]{2,1,0:T(8,128)S(1)}, u32[]{:S(2)}, u32[]{:S(2)}) collective-permute-start(f32[1,128,512]{2,1,0:T(8,128)S(1)} %get-tuple-element.39), channel_id=1, source_target_pairs={{0,4},{4,8},{8,12},{12,16},{16,20},{20,24},{24,28},{28,32},{32,36}... | collective-permute-start | bytes 786440 | tf_op jit(solution)/shard_map/ppermute | solution.py:29
  503.1 5.9 %collective-permute-start.14 = (f32[4,1,512]{2,1,0:T(1,128)S(1)}, f32[4,1,512]{2,1,0:T(1,128)S(1)}, u32[]{:S(2)}, u32[]{:S(2)}) collective-permute-start(f32[4,1,512]{2,1,0:T(1,128)S(1)} %get-tuple-element.42), channel_id=1, source_target_pairs={{1,0},{2,1},{3,2},{5,4},{6,5},{7,6},{9,8},{10,9},{11,10},{13,12},{... | collective-permute-start | bytes 24584 | tf_op jit(solution)/shard_map/ppermute | solution.py:30
  504.4 5.9 %collective-permute-start.15 = (f32[4,1,512]{2,1,0:T(1,128)S(1)}, f32[4,1,512]{2,1,0:T(1,128)S(1)}, u32[]{:S(2)}, u32[]{:S(2)}) collective-permute-start(f32[4,1,512]{2,1,0:T(1,128)S(1)} %get-tuple-element.41), channel_id=1, source_target_pairs={{0,1},{1,2},{2,3},{4,5},{5,6},{6,7},{8,9},{9,10},{10,11},{12,13},{... | collective-permute-start | bytes 24584 | tf_op jit(solution)/shard_map/ppermute | solution.py:29
  554.7 3.5 copy-start.1
